TPU v7x, 512 devices: a whole 4x4x16 slice. The times are simulated.
512 devices in a mesh: grp: 16 (over x, y_hi, core), ep: 32 (over y_lo, z).
Axes of the slice: x: 4, y: 4 (y_hi: 2, y_lo: 2; y = y_hi * 2 + y_lo), z: 16, core: 2. Of those that a mesh axis runs over, the one named last changes fastest.
Arguments:
- tokens: bfloat16 [4096, 3584], P('ep', 'grp'), may hold values from -6 to 6
- routes: int32 [4096, 1], P('ep'), may hold values from 0 to 31; in each aligned block of 128 rows (0 to 127, 128 to 255, ...) at most 8 rows name the same one
- route_weights: float32 [4096, 1], P('ep'), may hold values from 0.2 to 1
- hot_experts: int32 [16], replicated, may hold values from 0 to 15, as said below
- w_gate: bfloat16 [16, 3584, 2048], P(None, 'ep', 'grp'), may hold values from -0.09375 to 0.09375
- w_up: bfloat16 [16, 3584, 2048], P(None, 'ep', 'grp'), may hold values from -0.09375 to 0.09375
- w_down: bfloat16 [16, 2048, 3584], P(None, 'grp', 'ep'), may hold values from -0.125 to 0.125
- cotangent: bfloat16 [4096, 3584], P('ep', 'grp'), may hold values from -3 to 3
Outputs:
- layer_output: bfloat16 [4096, 3584], P('ep', 'grp')
- grad_tokens: bfloat16 [4096, 3584], P('ep', 'grp')
- grad_gate: bfloat16 [16, 3584, 2048], P(None, 'ep', 'grp')
- grad_up: bfloat16 [16, 3584, 2048], P(None, 'ep', 'grp')
- grad_down: bfloat16 [16, 2048, 3584], P(None, 'grp', 'ep')
Inputs may be any that keep to these rules, and one draw needn't show every extreme that they name: `routes`: each row names one slot. Among the rows of one device (aligned blocks of 128 rows) no slot is named by more than 8 rows. `hot_experts`: entry j is the expert held by slot 16 + j; an expert may appear several times.
All inputs are finite; a program needn't handle non-finite values.
Results may differ from a plain program's by a relative error of at most 0.02.
Values may be sent and summed in bfloat16 or wider, within the bound.
A program may use at most 64 MiB of HBM per device.

v0:
```python
import jax
import jax.numpy as jnp
from jax import lax
from jax.sharding import PartitionSpec as P


def shards(tokens, routes, route_weights, hot_experts, w_gate, w_up, w_down, cotangent):
    ep_size = lax.axis_size("ep")
    tok_count = tokens.shape[0]
    top_count = routes.shape[1]
    flat_count = tok_count * top_count
    capacity = 2 * flat_count // ep_size
    pad_rows = ep_size * capacity
    expert_count = w_gate.shape[0]
    hidden = w_gate.shape[2]
    stored = w_gate.shape[1]
    width = stored * ep_size
    slot_host = jnp.concatenate([jnp.arange(expert_count, dtype=jnp.int32), hot_experts])
    flat_slot = routes.reshape(-1)
    onehot = (flat_slot[:, None] == jnp.arange(ep_size, dtype=jnp.int32)[None, :]).astype(jnp.int32)
    before = jnp.cumsum(onehot, axis=0) - onehot
    position = jnp.sum(before * onehot, axis=1)
    dest = flat_slot * capacity + position
    source = (
        jnp.full((pad_rows,), flat_count, jnp.int32)
        .at[dest]
        .set(jnp.arange(flat_count, dtype=jnp.int32))
    )
    token_of = source // top_count
    flat_weights = route_weights.reshape(-1)
    weight_of = jnp.take(jnp.concatenate([flat_weights, jnp.zeros((1,), jnp.float32)]), source)
    sel_gate = jnp.take(w_gate, slot_host, axis=0)
    sel_up = jnp.take(w_up, slot_host, axis=0)
    sel_down = jnp.swapaxes(jnp.take(w_down, slot_host, axis=0), 1, 2)
    packed = jnp.concatenate([sel_gate, sel_up, sel_down], axis=2)
    received = lax.all_to_all(packed, "ep", split_axis=0, concat_axis=0, tiled=True)
    slot_weights = received.reshape(width, 3 * hidden)
    gate_up_w = slot_weights[:, : 2 * hidden]
    down_t = slot_weights[:, 2 * hidden :]

    def pick_rows(source_table, route_scale):
        extended = jnp.concatenate(
            [source_table, jnp.zeros((1, source_table.shape[1]), source_table.dtype)], axis=0
        )
        picked = jnp.take(extended, token_of, axis=0)
        if route_scale is not None:
            picked = (picked.astype(jnp.float32) * route_scale[:, None]).astype(jnp.bfloat16)
        return picked

    def deliver(source_table, route_scale):
        send_rows = pick_rows(source_table, route_scale)
        moved = lax.all_to_all(
            send_rows.reshape(ep_size, capacity, -1), "ep", split_axis=0, concat_axis=0, tiled=True
        )
        return lax.all_gather(moved.reshape(pad_rows, -1), "grp", axis=1, tiled=True)

    def combine(part_rows, weighted):
        block_sum = lax.psum_scatter(
            part_rows.astype(jnp.float32).astype(jnp.bfloat16),
            "grp",
            scatter_dimension=1,
            tiled=True,
        ).astype(jnp.float32)
        returned = lax.all_to_all(
            block_sum.reshape(ep_size, capacity, -1).astype(jnp.bfloat16),
            "ep",
            split_axis=0,
            concat_axis=0,
            tiled=True,
        ).astype(jnp.float32)
        route_rows = jnp.take(returned.reshape(pad_rows, -1), dest, axis=0)
        if weighted:
            route_rows = route_rows * flat_weights[:, None]
        return jnp.sum(route_rows.reshape(tok_count, top_count, -1), axis=1)

    contract_last = (((1,), (1,)), ((), ()))
    contract_first = (((0,), (0,)), ((), ()))
    x_rows = deliver(tokens, None)
    gate_up = jnp.dot(x_rows, gate_up_w, preferred_element_type=jnp.float32)
    gate_pre = gate_up[:, :hidden]
    up_pre = gate_up[:, hidden:]
    sigmoid_gate = jax.nn.sigmoid(gate_pre)
    act = (gate_pre * sigmoid_gate * up_pre).astype(jnp.bfloat16)
    out_parts = lax.dot_general(
        act, down_t, contract_last, preferred_element_type=jnp.float32
    ).astype(jnp.bfloat16)
    layer_output = combine(out_parts, True).astype(jnp.bfloat16)
    dz_rows = deliver(cotangent, weight_of)
    act_grad = jnp.dot(dz_rows, down_t, preferred_element_type=jnp.float32)
    gate_grad = act_grad * up_pre * sigmoid_gate * (1.0 + gate_pre * (1.0 - sigmoid_gate))
    up_grad = act_grad * gate_pre * sigmoid_gate
    pre_grad = jnp.concatenate([gate_grad, up_grad], axis=1).astype(jnp.bfloat16)
    tok_parts = lax.dot_general(
        pre_grad, gate_up_w, contract_last, preferred_element_type=jnp.float32
    ).astype(jnp.bfloat16)
    grad_tokens = combine(tok_parts, False).astype(jnp.bfloat16)
    grad_gate_up = lax.dot_general(
        x_rows, pre_grad, contract_first, preferred_element_type=jnp.float32
    )
    grad_down_t = lax.dot_general(dz_rows, act, contract_first, preferred_element_type=jnp.float32)
    slot_grad = jnp.concatenate([grad_gate_up, grad_down_t], axis=1).astype(jnp.bfloat16)
    owner_pieces = lax.all_to_all(
        slot_grad.reshape(ep_size, stored, 3 * hidden),
        "ep",
        split_axis=0,
        concat_axis=0,
        tiled=True,
    )
    host_onehot = (slot_host[None, :] == jnp.arange(expert_count, dtype=jnp.int32)[:, None]).astype(
        jnp.bfloat16
    )
    totals = jnp.einsum(
        "es,sdh->edh", host_onehot, owner_pieces, preferred_element_type=jnp.float32
    )
    grad_gate = totals[:, :, :hidden].astype(jnp.bfloat16)
    grad_up = totals[:, :, hidden : 2 * hidden].astype(jnp.bfloat16)
    grad_down = jnp.swapaxes(totals[:, :, 2 * hidden :], 1, 2).astype(jnp.bfloat16)
    return (layer_output, grad_tokens, grad_gate, grad_up, grad_down)


def solution(mesh):
    placed = (
        P("ep", "grp"),
        P("ep", None),
        P("ep", None),
        P(),
        P(None, "ep", "grp"),
        P(None, "ep", "grp"),
        P(None, "grp", "ep"),
        P("ep", "grp"),
    )
    return jax.shard_map(
        shards,
        mesh=mesh,
        in_specs=placed,
        out_specs=(
            P("ep", "grp"),
            P("ep", "grp"),
            P(None, "ep", "grp"),
            P(None, "ep", "grp"),
            P(None, "grp", "ep"),
        ),
        check_vma=False,
    )
```

profile of v0, /device:TPU:32, one launch (start us, length us, event | category | flops | bytes accessed | tf_op | source)
XLA Modules:
  0.0 573.1 jit_solution(13646672877807859614)
XLA Ops:
  11.4 1.9 gather_fusion.1
  14.3 1.2 gather_fusion.2
  16.2 16.4 %all-to-all-start = ((bf16[32,8,224]{2,1,0:T(8,128)(2,1)}), bf16[32,8,224]{2,1,0:T(8,128)(2,1)S(1)}, u32[]{:S(2)}, u32[]{:S(2)}) async-start(bf16[32,8,224]{2,1,0:T(8,128)(2,1)} %select_bitcast_fusion.1), calls=%async_computation | async-start | bytes 262144 | tf_op jit(solution)/shard_map/all_to_all | solution.py:52
  34.4 1.2 gather_fusion.6
  35.5 1.7 gather_fusion
  38.1 1.5 broadcast_select_fusion.1
  39.6 8.8 %all-to-all-done = bf16[32,8,224]{2,1,0:T(8,128)(2,1)S(1)} async-done(((bf16[32,8,224]{2,1,0:T(8,128)(2,1)}), bf16[32,8,224]{2,1,0:T(8,128)(2,1)S(1)}, u32[]{:S(2)}, u32[]{:S(2)}) %all-to-all-start) | async-done | bytes 114720 | tf_op jit(solution)/shard_map/all_to_all | solution.py:52
  48.4 4.7 all-to-all-start.3
  53.3 3.4 pad_maximum_fusion
  56.7 11.4 %all-to-all-done.3 = bf16[32,8,224]{2,1,0:T(8,128)(2,1)S(1)} async-done(((bf16[32,8,224]{2,1,0:T(8,128)(2,1)}), bf16[32,8,224]{2,1,0:T(8,128)(2,1)S(1)}, u32[]{:S(2)}, u32[]{:S(2)}) %all-to-all-start.3) | async-done | bytes 114720 | tf_op jit(solution)/shard_map/all_to_all | solution.py:52
  68.1 4.9 all-to-all-start.1
  74.8 69.1 %all-gather.3.cloned.1.call-done = bf16[256,3584]{0,1:T(8,128)(2,1)} async-done(((bf16[256,224]{0,1:T(8,128)(2,1)}), bf16[256,3584]{0,1:T(8,128)(2,1)}) %all-gather.3.cloned.1.call-update) | async-done | bytes 1835024 | tf_op jit(solution)/shard_map/all_gather | solution.py:55
  143.9 53.7 %all-to-all-done.1 = bf16[32,112,384]{2,1,0:T(8,128)(2,1)S(1)} async-done(((bf16[32,112,384]{2,1,0:T(8,128)(2,1)}), bf16[32,112,384]{2,1,0:T(8,128)(2,1)S(1)}, u32[]{:S(2)}, u32[]{:S(2)}) %all-to-all-start.1) | async-done | bytes 2752544 | tf_op jit(solution)/shard_map/all_to_all | solution.py:36
  197.6 3.0 fusion.6
  200.6 10.0 %all-gather.5.cloned.1.call-done = bf16[256,3584]{0,1:T(8,128)(2,1)} async-done(((bf16[256,224]{0,1:T(8,128)(2,1)}), bf16[256,3584]{0,1:T(8,128)(2,1)}) %all-gather.5.cloned.1.call-update) | async-done | bytes 1835024 | tf_op jit(solution)/shard_map/all_gather | solution.py:55
  210.6 2.1 multiply_convert_fusion.2
  212.7 1.9 convolution_convert_fusion.1
  214.7 1.9 convolution_convert_fusion
  216.6 89.9 %reduce-scatter.5.cloned.1.call-done = bf16[256,224]{0,1:T(8,128)(2,1)} async-done(((bf16[256,3584]{0,1:T(8,128)(2,1)}), bf16[256,224]{0,1:T(8,128)(2,1)}) %reduce-scatter.5.cloned.1.call-update) | async-done | bytes 114704 | tf_op jit(solution)/shard_map/reduce_scatter | solution.py:58
  306.5 1.7 copy.52
  308.2 13.0 %all-to-all-start.4 = ((bf16[32,8,224]{2,1,0:T(8,128)(2,1)}), bf16[32,8,224]{2,1,0:T(8,128)(2,1)S(1)}, u32[]{:S(2)}, u32[]{:S(2)}) async-start(bf16[32,8,224]{2,1,0:T(8,128)(2,1)} %bitcast.14), calls=%async_computation.6 | async-start | bytes 262144 | tf_op jit(solution)/shard_map/all_to_all | solution.py:64
  321.2 2.2 convolution_convert_fusion.2
  323.3 80.7 %reduce-scatter.3.cloned.1.call-done = bf16[256,224]{0,1:T(8,128)(2,1)} async-done(((bf16[256,3584]{0,1:T(8,128)(2,1)}), bf16[256,224]{0,1:T(8,128)(2,1)}) %reduce-scatter.3.cloned.1.call-update) | async-done | bytes 114704 | tf_op jit(solution)/shard_map/reduce_scatter | solution.py:58
  404.1 1.7 copy.49
  405.7 13.0 %all-to-all-start.2 = ((bf16[32,8,224]{2,1,0:T(8,128)(2,1)}), bf16[32,8,224]{2,1,0:T(8,128)(2,1)S(1)}, u32[]{:S(2)}, u32[]{:S(2)}) async-start(bf16[32,8,224]{2,1,0:T(8,128)(2,1)} %bitcast.9), calls=%async_computation.3 | async-start | bytes 262144 | tf_op jit(solution)/shard_map/all_to_all | solution.py:64
  418.8 2.1 convolution_convert_fusion.3
  420.9 1.8 pad_maximum_fusion.1
  422.7 10.6 %all-to-all-done.2 = bf16[32,8,224]{2,1,0:T(8,128)(2,1)S(1)} async-done(((bf16[32,8,224]{2,1,0:T(8,128)(2,1)}), bf16[32,8,224]{2,1,0:T(8,128)(2,1)S(1)}, u32[]{:S(2)}, u32[]{:S(2)}) %all-to-all-start.2) | async-done | bytes 114720 | tf_op jit(solution)/shard_map/all_to_all | solution.py:64
  434.0 4.9 all-to-all-start.5
  441.6 1.4 gather_fusion.5
  443.0 1.0 fusion.12
  444.7 118.4 %all-to-all-done.5 = bf16[32,112,384]{2,1,0:T(8,128)(2,1)S(1)} async-done(((bf16[32,112,384]{2,1,0:T(8,128)(2,1)}), bf16[32,112,384]{2,1,0:T(8,128)(2,1)S(1)}, u32[]{:S(2)}, u32[]{:S(2)}) %all-to-all-start.5) | async-done | bytes 2752544 | tf_op jit(solution)/shard_map/all_to_all | solution.py:102
  (63 shorter events, 17.7 us)
Async XLA Ops:
  7.2 25.5 %copy-start = (bf16[16,112,128]{2,1,0:T(8,128)(2,1)S(1)}, bf16[16,112,128]{2,1,0:T(8,128)(2,1)}, u32[]{:S(2)}) copy-start(bf16[16,112,128]{2,1,0:T(8,128)(2,1)} %param.19) | copy-start | bytes 1376260
  7.2 25.4 %copy-start.6 = (s32[16]{0:T(128)S(1)}, s32[16]{0:T(128)}, u32[]{:S(2)}) copy-start(s32[16]{0:T(128)} %param.17) | copy-start | bytes 196
  7.2 26.2 %copy-start.1 = (bf16[16,112,128]{2,1,0:T(8,128)(2,1)S(1)}, bf16[16,112,128]{2,1,0:T(8,128)(2,1)}, u32[]{:S(2)}) copy-start(bf16[16,112,128]{2,1,0:T(8,128)(2,1)} %param.18) | copy-start | bytes 1376260
  14.3 20.0 %copy-start.3 = (bf16[128,224]{0,1:T(8,128)(2,1)S(1)}, bf16[128,224]{0,1:T(8,128)(2,1)}, u32[]{:S(2)}) copy-start(bf16[128,224]{0,1:T(8,128)(2,1)} %param.21) | copy-start | bytes 172036
  16.2 32.2 %all-to-all-start = ((bf16[32,8,224]{2,1,0:T(8,128)(2,1)}), bf16[32,8,224]{2,1,0:T(8,128)(2,1)S(1)}, u32[]{:S(2)}, u32[]{:S(2)}) async-start(bf16[32,8,224]{2,1,0:T(8,128)(2,1)} %select_bitcast_fusion.1), calls=%async_computation | async-start | bytes 262144 | tf_op jit(solution)/shard_map/all_to_all | solution.py:52
  48.4 19.7 %all-to-all-start.3 = ((bf16[32,8,224]{2,1,0:T(8,128)(2,1)}), bf16[32,8,224]{2,1,0:T(8,128)(2,1)S(1)}, u32[]{:S(2)}, u32[]{:S(2)}) async-start(bf16[32,8,224]{2,1,0:T(8,128)(2,1)} %fusion.11), calls=%async_computation.4 | async-start | bytes 262144 | tf_op jit(solution)/shard_map/all_to_all | solution.py:52
  68.1 129.4 %all-to-all-start.1 = ((bf16[32,112,384]{2,1,0:T(8,128)(2,1)}), bf16[32,112,384]{2,1,0:T(8,128)(2,1)S(1)}, u32[]{:S(2)}, u32[]{:S(2)}) async-start(bf16[32,112,384]{2,1,0:T(8,128)(2,1)} %pad_maximum_fusion), calls=%async_computation.1 | async-start | bytes 5505024 | tf_op jit(solution)/shard_map/all_to_all | solution.py:36
  73.1 70.8 %all-gather.3.cloned.1.call-start = ((), (), s32[]{:S(2)}) async-start(), calls=%async_computation.8 | async-start | bytes 1949696 | tf_op jit(solution)/shard_map/all_gather | solution.py:55
  73.9 136.8 %all-gather.5.cloned.1.call-start = ((), (), s32[]{:S(2)}) async-start(), calls=%async_computation.10 | async-start | bytes 1949696 | tf_op jit(solution)/shard_map/all_gather | solution.py:55
  74.7 231.8 %reduce-scatter.5.cloned.1.call-start = ((), (), s32[]{:S(2)}) async-start(), calls=%async_computation.11 | async-start | bytes 1949696 | tf_op jit(solution)/shard_map/reduce_scatter | solution.py:58
  214.7 189.4 %reduce-scatter.3.cloned.1.call-start = ((), (), s32[]{:S(2)}) async-start(), calls=%async_computation.9 | async-start | bytes 1949696 | tf_op jit(solution)/shard_map/reduce_scatter | solution.py:58
  308.2 97.5 %all-to-all-start.4 = ((bf16[32,8,224]{2,1,0:T(8,128)(2,1)}), bf16[32,8,224]{2,1,0:T(8,128)(2,1)S(1)}, u32[]{:S(2)}, u32[]{:S(2)}) async-start(bf16[32,8,224]{2,1,0:T(8,128)(2,1)} %bitcast.14), calls=%async_computation.6 | async-start | bytes 262144 | tf_op jit(solution)/shard_map/all_to_all | solution.py:64
  405.7 27.6 %all-to-all-start.2 = ((bf16[32,8,224]{2,1,0:T(8,128)(2,1)}), bf16[32,8,224]{2,1,0:T(8,128)(2,1)S(1)}, u32[]{:S(2)}, u32[]{:S(2)}) async-start(bf16[32,8,224]{2,1,0:T(8,128)(2,1)} %bitcast.9), calls=%async_computation.3 | async-start | bytes 262144 | tf_op jit(solution)/shard_map/all_to_all | solution.py:64
  422.7 16.2 %copy-start.4 = (s32[128,1]{0,1:T(1,128)S(1)}, s32[128,1]{0,1:T(1,128)}, u32[]{:S(2)}) copy-start(s32[128,1]{0,1:T(1,128)} %param.15) | copy-start | bytes 1540
  422.7 20.3 %copy-start.5 = (f32[128,1]{0,1:T(1,128)S(1)}, f32[128,1]{0,1:T(1,128)}, u32[]{:S(2)}) copy-start(f32[128,1]{0,1:T(1,128)} %param.16) | copy-start | bytes 1540
  433.3 0.7 copy-start.2
  434.0 129.1 %all-to-all-start.5 = ((bf16[32,112,384]{2,1,0:T(8,128)(2,1)}), bf16[32,112,384]{2,1,0:T(8,128)(2,1)S(1)}, u32[]{:S(2)}, u32[]{:S(2)}) async-start(bf16[32,112,384]{2,1,0:T(8,128)(2,1)} %pad_maximum_fusion.1), calls=%async_computation.7 | async-start | bytes 5505024 | tf_op jit(solution)/shard_map/all_to_all | solution.py:102
Sparse Core Ops, SparseCore 0:
  77.7 66.0 all-gather.2
  147.7 62.8 all-gather.4
  215.4 91.0 reduce-scatter.4
  311.9 92.1 reduce-scatter.2
where the time goes:
time: 574 us; the launch traced here: 573 us
  waiting for transfers between devices  453 us (79%)
  starting transfers between devices  57.1 us (10%)
  local copies, waits for them, and re-layouts  21.6 us (4%)
  between operations  14.1 us (2%)
  other arithmetic  13.8 us (2%)
  matrix products  13.8 us (2%)
    reduce_scatter x2, waiting for transfers between devices, combine(): lax.psum_scatter(part_rows.astype(jnp.float32).astype(jnp.bfloat16), 'grp...  171 us
    all_to_all x1, waiting for transfers between devices, shards(): lax.all_to_all(slot_grad.reshape(ep_size, stored, 3 * hidden), 'ep', spli...  118 us
    all_gather x2, waiting for transfers between devices, deliver(): lax.all_gather(moved.reshape(pad_rows, -1), 'grp', axis=1, tiled=True)  79.1 us
    all_to_all x1, waiting for transfers between devices, shards(): lax.all_to_all(packed, 'ep', split_axis=0, concat_axis=0, tiled=True)  53.7 us
    all_to_all x2, starting transfers between devices, combine(): lax.all_to_all(block_sum.reshape(ep_size, capacity, -1).astype(jnp.bfloat...  26 us
    all_to_all x2, starting transfers between devices, deliver(): lax.all_to_all(send_rows.reshape(ep_size, capacity, -1), 'ep', split_axis...  21.1 us
    all_to_all x2, waiting for transfers between devices, deliver(): lax.all_to_all(send_rows.reshape(ep_size, capacity, -1), 'ep', split_axis...  20.2 us
  transfers between devices with their start and end apart: 10, of which 9 were waited for; matrix products, arithmetic and copies ran while one was open for 6% of the time, Pallas kernels for 0%

commit v1 on v0

--- a/solution.py
+++ b/solution.py
@@ -2,6 +2,13 @@
 import jax.numpy as jnp
 from jax import lax
 from jax.sharding import PartitionSpec as P
+
+
+def all_by_exchange(shard, name, dim):
+    peers = lax.axis_size(name)
+    blocks = jnp.stack([shard for _ in range(peers)])
+    blocks = lax.all_to_all(blocks, name, split_axis=0, concat_axis=0)
+    return jnp.concatenate(blocks, axis=dim)
 
 
 def shards(tokens, routes, route_weights, hot_experts, w_gate, w_up, w_down, cotangent):
@@ -52,7 +59,7 @@
         moved = lax.all_to_all(
             send_rows.reshape(ep_size, capacity, -1), "ep", split_axis=0, concat_axis=0, tiled=True
         )
-        return lax.all_gather(moved.reshape(pad_rows, -1), "grp", axis=1, tiled=True)
+        return all_by_exchange(moved.reshape(pad_rows, -1), "grp", 1)
 
     def combine(part_rows, weighted):
         block_sum = lax.psum_scatter(

time: 574 us -> 625 us (1.089)
  waiting for transfers between devices: 453 us -> 486 us
  starting transfers between devices: 57.1 us -> 69.9 us
  local copies, waits for them, and re-layouts: 21.6 us -> 28.7 us
    all_gather x2 -> x0, waiting for transfers between devices: 79.1 us -> none  [deliver(): lax.all_gather(moved.reshape(pad_rows, -1), 'grp', axis=1, tiled=True)]
    all_to_all x1, waiting for transfers between devices: 53.7 us -> 127 us  [shards(): lax.all_to_all(packed, 'ep', split_axis=0, concat_axis=0, tiled=True)]
    all_to_all x0 -> x2, waiting for transfers between devices: none -> 40.9 us  [all_by_exchange(): blocks = lax.all_to_all(blocks, name, split_axis=0, concat_axis=0)]
    all_to_all x0 -> x2, starting transfers between devices: none -> 12.8 us  [all_by_exchange(): blocks = lax.all_to_all(blocks, name, split_axis=0, concat_axis=0)]
    reduce_scatter x2, waiting for transfers between devices: 171 us -> 162 us  [combine(): lax.psum_scatter(part_rows.astype(jnp.float32).astype(jnp.bfloat16), 'grp...]
    all_to_all x2, waiting for transfers between devices: 20.2 us -> 28.3 us  [deliver(): lax.all_to_all(send_rows.reshape(ep_size, capacity, -1), 'ep', split_axis...]
  transfers between devices with their start and end apart: 10 -> 10, of which waited for: 9 -> 9; matrix products, arithmetic and copies ran while one was open for 6% -> 5% of each run, Pallas kernels for 0% -> 0%
where the time goes in v1:
time: 625 us; the launch traced here: 624 us
  waiting for transfers between devices  486 us (78%)
  starting transfers between devices  69.9 us (11%)
  local copies, waits for them, and re-layouts  28.7 us (5%)
  between operations  14.4 us (2%)
  matrix products  14 us (2%)
  other arithmetic  11 us (2%)
    reduce_scatter x2, waiting for transfers between devices, combine(): lax.psum_scatter(part_rows.astype(jnp.float32).astype(jnp.bfloat16), 'grp...  162 us
    all_to_all x1, waiting for transfers between devices, shards(): lax.all_to_all(packed, 'ep', split_axis=0, concat_axis=0, tiled=True)  127 us
    all_to_all x1, waiting for transfers between devices, shards(): lax.all_to_all(slot_grad.reshape(ep_size, stored, 3 * hidden), 'ep', spli...  118 us
    all_to_all x2, waiting for transfers between devices, all_by_exchange(): blocks = lax.all_to_all(blocks, name, split_axis=0, concat_axis=0)  40.9 us
    all_to_all x2, waiting for transfers between devices, deliver(): lax.all_to_all(send_rows.reshape(ep_size, capacity, -1), 'ep', split_axis...  28.3 us
    all_to_all x2, starting transfers between devices, combine(): lax.all_to_all(block_sum.reshape(ep_size, capacity, -1).astype(jnp.bfloat...  26 us
    all_to_all x2, starting transfers between devices, deliver(): lax.all_to_all(send_rows.reshape(ep_size, capacity, -1), 'ep', split_axis...  21.1 us
    all_to_all x2, starting transfers between devices, all_by_exchange(): blocks = lax.all_to_all(blocks, name, split_axis=0, concat_axis=0)  12.8 us
  transfers between devices with their start and end apart: 10, of which 9 were waited for; matrix products, arithmetic and copies ran while one was open for 5% of the time, Pallas kernels for 0%

profile of v1, /device:TPU:32, one launch (start us, length us, event | category | flops | bytes accessed | tf_op | source)
XLA Modules:
  0.0 624.2 jit_solution(3833078991277965114)
XLA Ops:
  11.4 1.9 gather_fusion.1
  16.2 16.4 %all-to-all-start = ((bf16[32,8,224]{2,1,0:T(8,128)(2,1)}), bf16[32,8,224]{2,1,0:T(8,128)(2,1)S(1)}, u32[]{:S(2)}, u32[]{:S(2)}) async-start(bf16[32,8,224]{2,1,0:T(8,128)(2,1)} %select_bitcast_fusion.1), calls=%async_computation | async-start | bytes 262144 | tf_op jit(solution)/shard_map/all_to_all | solution.py:59
  34.6 13.8 %all-to-all-done = bf16[32,8,224]{2,1,0:T(8,128)(2,1)S(1)} async-done(((bf16[32,8,224]{2,1,0:T(8,128)(2,1)}), bf16[32,8,224]{2,1,0:T(8,128)(2,1)S(1)}, u32[]{:S(2)}, u32[]{:S(2)}) %all-to-all-start) | async-done | bytes 114720 | tf_op jit(solution)/shard_map/all_to_all | solution.py:59
  48.4 4.7 all-to-all-start.4
  53.3 14.5 %all-to-all-done.4 = bf16[32,8,224]{2,1,0:T(8,128)(2,1)S(1)} async-done(((bf16[32,8,224]{2,1,0:T(8,128)(2,1)}), bf16[32,8,224]{2,1,0:T(8,128)(2,1)S(1)}, u32[]{:S(2)}, u32[]{:S(2)}) %all-to-all-start.4) | async-done | bytes 114720 | tf_op jit(solution)/shard_map/all_to_all | solution.py:59
  69.3 6.9 %all-to-all-start.1 = ((bf16[16,256,224]{1,2,0:T(8,128)(2,1)}), bf16[16,256,224]{1,2,0:T(8,128)(2,1)S(1)}, u32[]{:S(2)}, u32[]{:S(2)}) async-start(bf16[16,256,224]{1,2,0:T(8,128)(2,1)} %stack.6), calls=%async_computation.1 | async-start | bytes 3670016 | tf_op jit(solution)/shard_map/all_to_all | solution.py:10
  76.2 1.6 gather_fusion.4
  77.8 1.6 gather_fusion.3
  79.5 1.7 gather_fusion
  81.5 1.7 broadcast_select_fusion.1
  83.2 1.9 pad_maximum_fusion
  85.1 17.5 %all-to-all-done.1 = bf16[16,256,224]{1,2,0:T(8,128)(2,1)S(1)} async-done(((bf16[16,256,224]{1,2,0:T(8,128)(2,1)}), bf16[16,256,224]{1,2,0:T(8,128)(2,1)S(1)}, u32[]{:S(2)}, u32[]{:S(2)}) %all-to-all-start.1) | async-done | bytes 1835040 | tf_op jit(solution)/shard_map/all_to_all | solution.py:10
  103.8 5.0 all-to-all-start.2
  108.8 127.3 %all-to-all-done.2 = bf16[32,112,384]{2,1,0:T(8,128)(2,1)S(1)} async-done(((bf16[32,112,384]{2,1,0:T(8,128)(2,1)}), bf16[32,112,384]{2,1,0:T(8,128)(2,1)S(1)}, u32[]{:S(2)}, u32[]{:S(2)}) %all-to-all-start.2) | async-done | bytes 2752544 | tf_op jit(solution)/shard_map/all_to_all | solution.py:43
  237.6 5.9 all-to-all-start.5
  243.6 3.0 fusion.13
  246.6 23.4 %all-to-all-done.5 = bf16[16,256,224]{1,2,0:T(8,128)(2,1)} async-done(((bf16[16,256,224]{1,2,0:T(8,128)(2,1)}), bf16[16,256,224]{1,2,0:T(8,128)(2,1)}, u32[]{:S(2)}, u32[]{:S(2)}) %all-to-all-start.5) | async-done | bytes 1835040 | tf_op jit(solution)/shard_map/all_to_all | solution.py:10
  270.0 2.1 multiply_convert_fusion.2
  272.1 1.9 convolution_convert_fusion.1
  274.1 1.9 convolution_convert_fusion
  276.0 81.2 %reduce-scatter.5.cloned.1.call-done = bf16[256,224]{0,1:T(8,128)(2,1)} async-done(((bf16[256,3584]{0,1:T(8,128)(2,1)}), bf16[256,224]{0,1:T(8,128)(2,1)}) %reduce-scatter.5.cloned.1.call-update) | async-done | bytes 114704 | tf_op jit(solution)/shard_map/reduce_scatter | solution.py:65
  357.2 1.7 copy.38
  358.8 13.0 %all-to-all-start.6 = ((bf16[32,8,224]{2,1,0:T(8,128)(2,1)}), bf16[32,8,224]{2,1,0:T(8,128)(2,1)S(1)}, u32[]{:S(2)}, u32[]{:S(2)}) async-start(bf16[32,8,224]{2,1,0:T(8,128)(2,1)} %bitcast.18), calls=%async_computation.8 | async-start | bytes 262144 | tf_op jit(solution)/shard_map/all_to_all | solution.py:71
  371.8 2.3 fusion.6
  374.1 80.8 %reduce-scatter.3.cloned.1.call-done = bf16[256,224]{0,1:T(8,128)(2,1)} async-done(((bf16[256,3584]{0,1:T(8,128)(2,1)}), bf16[256,224]{0,1:T(8,128)(2,1)}) %reduce-scatter.3.cloned.1.call-update) | async-done | bytes 114704 | tf_op jit(solution)/shard_map/reduce_scatter | solution.py:65
  454.9 1.7 copy.35
  456.6 13.0 %all-to-all-start.3 = ((bf16[32,8,224]{2,1,0:T(8,128)(2,1)}), bf16[32,8,224]{2,1,0:T(8,128)(2,1)S(1)}, u32[]{:S(2)}, u32[]{:S(2)}) async-start(bf16[32,8,224]{2,1,0:T(8,128)(2,1)} %bitcast.11), calls=%async_computation.4 | async-start | bytes 262144 | tf_op jit(solution)/shard_map/all_to_all | solution.py:71
  469.6 2.2 fusion.15
  472.1 2.5 copy.43
  474.7 9.5 %all-to-all-done.3 = bf16[32,8,224]{2,1,0:T(8,128)(2,1)S(1)} async-done(((bf16[32,8,224]{2,1,0:T(8,128)(2,1)}), bf16[32,8,224]{2,1,0:T(8,128)(2,1)S(1)}, u32[]{:S(2)}, u32[]{:S(2)}) %all-to-all-start.3) | async-done | bytes 114720 | tf_op jit(solution)/shard_map/all_to_all | solution.py:71
  484.8 4.9 all-to-all-start.7
  495.5 118.4 %all-to-all-done.7 = bf16[32,112,384]{2,1,0:T(8,128)(2,1)S(1)} async-done(((bf16[32,112,384]{2,1,0:T(8,128)(2,1)}), bf16[32,112,384]{2,1,0:T(8,128)(2,1)S(1)}, u32[]{:S(2)}, u32[]{:S(2)}) %all-to-all-start.7) | async-done | bytes 2752544 | tf_op jit(solution)/shard_map/all_to_all | solution.py:109
  (66 shorter events, 24.0 us)
Async XLA Ops:
  7.2 69.1 %copy-start = (bf16[16,112,128]{2,1,0:T(8,128)(2,1)S(1)}, bf16[16,112,128]{2,1,0:T(8,128)(2,1)}, u32[]{:S(2)}) copy-start(bf16[16,112,128]{2,1,0:T(8,128)(2,1)} %param.19) | copy-start | bytes 1376260
  7.2 25.4 %copy-start.4 = (bf16[128,224]{0,1:T(8,128)(2,1)S(1)}, bf16[128,224]{0,1:T(8,128)(2,1)}, u32[]{:S(2)}) copy-start(bf16[128,224]{0,1:T(8,128)(2,1)} %param.21) | copy-start | bytes 172036
  16.2 32.2 %all-to-all-start = ((bf16[32,8,224]{2,1,0:T(8,128)(2,1)}), bf16[32,8,224]{2,1,0:T(8,128)(2,1)S(1)}, u32[]{:S(2)}, u32[]{:S(2)}) async-start(bf16[32,8,224]{2,1,0:T(8,128)(2,1)} %select_bitcast_fusion.1), calls=%async_computation | async-start | bytes 262144 | tf_op jit(solution)/shard_map/all_to_all | solution.py:59
  48.4 19.4 %all-to-all-start.4 = ((bf16[32,8,224]{2,1,0:T(8,128)(2,1)}), bf16[32,8,224]{2,1,0:T(8,128)(2,1)S(1)}, u32[]{:S(2)}, u32[]{:S(2)}) async-start(bf16[32,8,224]{2,1,0:T(8,128)(2,1)} %fusion.21), calls=%async_computation.5 | async-start | bytes 262144 | tf_op jit(solution)/shard_map/all_to_all | solution.py:59
  53.3 22.9 %copy-start.7 = (s32[16]{0:T(128)S(1)}, s32[16]{0:T(128)}, u32[]{:S(2)}) copy-start(s32[16]{0:T(128)} %param.17) | copy-start | bytes 196
  69.3 8.6 %copy-start.2 = (bf16[16,112,128]{2,1,0:T(8,128)(2,1)S(1)}, bf16[16,112,128]{2,1,0:T(8,128)(2,1)}, u32[]{:S(2)}) copy-start(bf16[16,112,128]{2,1,0:T(8,128)(2,1)} %param.18) | copy-start | bytes 1376260
  69.3 33.3 %all-to-all-start.1 = ((bf16[16,256,224]{1,2,0:T(8,128)(2,1)}), bf16[16,256,224]{1,2,0:T(8,128)(2,1)S(1)}, u32[]{:S(2)}, u32[]{:S(2)}) async-start(bf16[16,256,224]{1,2,0:T(8,128)(2,1)} %stack.6), calls=%async_computation.1 | async-start | bytes 3670016 | tf_op jit(solution)/shard_map/all_to_all | solution.py:10
  102.5 1.2 copy-start.1
  103.8 132.4 %all-to-all-start.2 = ((bf16[32,112,384]{2,1,0:T(8,128)(2,1)}), bf16[32,112,384]{2,1,0:T(8,128)(2,1)S(1)}, u32[]{:S(2)}, u32[]{:S(2)}) async-start(bf16[32,112,384]{2,1,0:T(8,128)(2,1)} %pad_maximum_fusion), calls=%async_computation.2 | async-start | bytes 5505024 | tf_op jit(solution)/shard_map/all_to_all | solution.py:43
  237.6 32.4 %all-to-all-start.5 = ((bf16[16,256,224]{1,2,0:T(8,128)(2,1)}), bf16[16,256,224]{1,2,0:T(8,128)(2,1)}, u32[]{:S(2)}, u32[]{:S(2)}) async-start(bf16[16,256,224]{1,2,0:T(8,128)(2,1)} %stack.7), calls=%async_computation.6 | async-start | bytes 3670016 | tf_op jit(solution)/shard_map/all_to_all | solution.py:10
  243.6 113.6 %reduce-scatter.5.cloned.1.call-start = ((), (), s32[]{:S(2)}) async-start(), calls=%async_computation.11 | async-start | bytes 1949696 | tf_op jit(solution)/shard_map/reduce_scatter | solution.py:65
  274.1 180.8 %reduce-scatter.3.cloned.1.call-start = ((), (), s32[]{:S(2)}) async-start(), calls=%async_computation.10 | async-start | bytes 1949696 | tf_op jit(solution)/shard_map/reduce_scatter | solution.py:65
  358.8 97.7 %all-to-all-start.6 = ((bf16[32,8,224]{2,1,0:T(8,128)(2,1)}), bf16[32,8,224]{2,1,0:T(8,128)(2,1)S(1)}, u32[]{:S(2)}, u32[]{:S(2)}) async-start(bf16[32,8,224]{2,1,0:T(8,128)(2,1)} %bitcast.18), calls=%async_computation.8 | async-start | bytes 262144 | tf_op jit(solution)/shard_map/all_to_all | solution.py:71
  456.6 27.6 %all-to-all-start.3 = ((bf16[32,8,224]{2,1,0:T(8,128)(2,1)}), bf16[32,8,224]{2,1,0:T(8,128)(2,1)S(1)}, u32[]{:S(2)}, u32[]{:S(2)}) async-start(bf16[32,8,224]{2,1,0:T(8,128)(2,1)} %bitcast.11), calls=%async_computation.4 | async-start | bytes 262144 | tf_op jit(solution)/shard_map/all_to_all | solution.py:71
  474.7 15.1 %copy-start.5 = (s32[128,1]{0,1:T(1,128)S(1)}, s32[128,1]{0,1:T(1,128)}, u32[]{:S(2)}) copy-start(s32[128,1]{0,1:T(1,128)} %param.15) | copy-start | bytes 1540
  474.7 19.1 %copy-start.6 = (f32[128,1]{0,1:T(1,128)S(1)}, f32[128,1]{0,1:T(1,128)}, u32[]{:S(2)}) copy-start(f32[128,1]{0,1:T(1,128)} %param.16) | copy-start | bytes 1540
  484.1 0.7 copy-start.3
  484.8 129.1 %all-to-all-start.7 = ((bf16[32,112,384]{2,1,0:T(8,128)(2,1)}), bf16[32,112,384]{2,1,0:T(8,128)(2,1)S(1)}, u32[]{:S(2)}, u32[]{:S(2)}) async-start(bf16[32,112,384]{2,1,0:T(8,128)(2,1)} %copy.43), calls=%async_computation.9 | async-start | bytes 5505024 | tf_op jit(solution)/shard_map/all_to_all | solution.py:109
Sparse Core Ops, SparseCore 0:
  274.2 82.9 reduce-scatter.4
  362.7 92.1 reduce-scatter.2
